TPU v7x, 32 devices: a whole 2x2x4 slice. The times are simulated.
32 devices in a mesh: grp: 4 (over y, x), dev: 8 (over z, core).
Axes of the slice: x: 2, y: 2, z: 4, core: 2. Of those that a mesh axis runs over, the one named last changes fastest.
Arguments:
- embeds: bfloat16 [3072, 1024], P(('grp', 'dev')), may hold values from -6 to 6
- cluster: int32 [3072], P(('grp', 'dev')), may hold values from 0 to 7, as said below
- priority: int32 [3072], P(('grp', 'dev')), may hold values from 0 to 3071, each once
Outputs:
- best: float32 [3072], P(('grp', 'dev'))
Inputs may be any that keep to these rules, and one draw needn't show every extreme that they name: `cluster`: cluster c belongs to group c // 2. Among the items of one device, at most 48 belong to the clusters of one group, and exactly 48 to some group. `priority`: each number appears once.
All inputs are finite; a program needn't handle non-finite values.
Results may differ from a plain program's by a relative error of at most 0.0013.
Values may be sent and summed in bfloat16 or wider, within the bound.
A program may use at most 128 MiB of HBM per device.

v0:
```python
import functools

import jax
import jax.numpy as jnp
from jax import lax
from jax.experimental import pallas as pl
from jax.experimental.pallas import tpu as pltpu
from jax.sharding import PartitionSpec as P

MESH = pl.DeviceIdType.MESH
LANES = 128


def batch_of(slots):
    return 0 if slots == 0 else 2 if slots % 2 == 0 else 1


def kernel(
    groups, layers, embeds_hbm, cluster_hbm, priority_hbm, out_ref,
    embeds_ref, cluster_ref, priority_ref,
    plane, normal, column, plane_key, column_key, plane_res, column_res, plane_got, column_got, total,
    own_res, partial, load_sem, plane_send, plane_recv, relay_send, relay_recv, pass_send, pass_recv,
    column_send, column_recv, plane_key_send, plane_key_recv, column_key_send, column_key_recv,
    plane_res_send, plane_res_recv, column_res_send, column_res_recv,
):
    items, width = embeds_ref.shape
    lanes = plane_key.shape[3]
    slots = layers // 2
    half = items // 2
    cut = width // 4 * 3
    parts = [(0, cut), (cut, width - cut)]
    lows = 2 if groups % 2 == 0 else 1
    highs = groups // lows
    batch = batch_of(slots)
    batches = slots // batch if slots else 1
    g, d = lax.axis_index("grp"), lax.axis_index("dev")
    z, c = d // 2, d % 2

    def at(group, layer, core):
        return {"grp": group, "dev": layer * 2 + core}

    def group_up(s):
        high, low = s // lows, s % lows
        return (g // lows + high) % highs * lows + (g % lows + low) % lows

    def group_down(s):
        high, low = s // lows, s % lows
        return (g // lows + highs - high) % highs * lows + (g % lows + lows - low) % lows

    def layer_up(s):
        return (z + s) % layers

    def core(k):
        return (c + k) % 2

    def sends(s):
        return (s % 2 == 0) & (z + s < layers) | (s % 2 == 1) & (z + s >= layers)

    def first_odd(layer):
        return layer + 1 + layer % 2

    def slot_of(s):
        to = layer_up(s)
        return (1 - s % 2) * (s // 2 - 1) + (s % 2) * (to // 2 + (s - first_odd(to)) // 2)

    def offset_of(j):
        return jnp.where(j < z // 2, 2 * (j + 1), first_odd(z) + 2 * (j - z // 2))

    def filled(j):
        return j < z // 2 + (layers + 1 - first_odd(z)) // 2

    def remote(src, dst, send, recv, device):
        return pltpu.make_async_remote_copy(
            src_ref=src, dst_ref=dst, send_sem=send, recv_sem=recv,
            device_id=device, device_id_type=MESH,
        )

    def each(start, count, body):
        if count <= 4:
            for i in range(start, count):
                body(i)
        else:
            lax.fori_loop(start, count, lambda i, carry: (body(i), carry)[1], 0)

    def each_if(start, count, test, body):
        each(start, count, lambda i: pl.when(test(i))(lambda: body(i)))

    near = [s for s in range(1, groups) if s < lows or s % lows == 0]
    far = [s for s in range(1, groups) if s not in near]
    every = [(s, k) for s in range(groups) for k in range(2)]
    peers = every[1:]

    def rows_of(h):
        return pl.ds(h * half, half)

    def plane_copy(s, h):
        return remote(embeds_hbm.at[rows_of(h)], plane.at[s, 0, rows_of(h)],
                      plane_send.at[s, h], plane_recv.at[s, h], at(group_up(s), z, c))

    def relay_copy(s, h):
        low, high = s % lows, s - s % lows
        source, way = (low, high) if h == 0 else (high, low)
        return remote(plane.at[source, 0, rows_of(h)], plane.at[s, 0, rows_of(h)],
                      relay_send.at[s, h], relay_recv.at[s, h], at(group_up(way), z, c))

    def pass_copy(s):
        return remote(plane.at[s, 0] if s else embeds_hbm, plane.at[s, 1],
                      pass_send.at[s], pass_recv.at[s], at(g, z, core(1)))

    def column_copy(s, j, h):
        columns = pl.ds(*parts[h])
        return remote(embeds_hbm.at[:, columns], column.at[j, :, columns],
                      column_send.at[s, h], column_recv.at[j, h], at(g, layer_up(s), c))

    def plane_key_copy(s, k):
        return remote(plane_key.at[0, 0], plane_key.at[s, k],
                      plane_key_send.at[s, k], plane_key_recv.at[s, k], at(group_up(s), z, core(k)))

    def column_key_copy(s, j):
        return remote(plane_key.at[0, 0], column_key.at[j],
                      column_key_send.at[s], column_key_recv.at[j], at(g, layer_up(s), c))

    def plane_res_copy(s, k):
        return remote(plane_res.at[s, k], plane_got.at[s, k],
                      plane_res_send.at[s, k], plane_res_recv.at[s, k], at(group_down(s), z, core(k)))

    def column_res_copy(j, s):
        return remote(column_res.at[j], column_got.at[s],
                      column_res_send.at[j], column_res_recv.at[s], at(g, (z + layers - s) % layers, c))

    loads = [
        pltpu.make_async_copy(src, dst, load_sem.at[i])
        for i, (src, dst) in enumerate(
            [(embeds_hbm, embeds_ref), (cluster_hbm, cluster_ref), (priority_hbm, priority_ref)]
        )
    ]
    for load in loads:
        load.start()

    barrier = pltpu.get_barrier_semaphore()

    def greet(device):
        pl.semaphore_signal(barrier, inc=1, device_id=device, device_id_type=MESH)

    column_key[...] = jnp.full(column_key.shape, -2.0, jnp.float32)
    each(1, layers, lambda s: greet(at(g, layer_up(s), c)))
    for s, k in peers:
        greet(at(group_up(s), z, core(k)))

    pl.semaphore_wait(barrier, len(peers) + layers - 1)

    def first_half(s):
        return 0 if s < lows else 1

    for i in range(2):
        each_if(1, layers, sends, lambda s: column_copy(s, slot_of(s), i).start())
        for s in near:
            plane_copy(s, first_half(s) if i == 0 else 1 - first_half(s)).start()
    pass_copy(0).start()

    total[...] = jnp.full(total.shape, -1.0, jnp.float32)
    plane_key[0, 0] = jnp.full((8, lanes), -1.0, jnp.float32)
    for load in loads:
        load.wait()
    values = embeds_ref[...].astype(jnp.float32)
    scale = lax.rsqrt(jnp.sum(values * values, axis=1, keepdims=True) + 1e-06)
    normal[0, 0] = (values * scale).astype(jnp.bfloat16)
    plane_key[0, 0, 0:1, :items] = cluster_ref[...].reshape(1, items).astype(jnp.float32)
    plane_key[0, 0, 1:2, :items] = priority_ref[...].reshape(1, items).astype(jnp.float32)
    plane_key[0, 0, 2:3, :items] = jnp.broadcast_to(scale, (items, LANES)).T[0:1]
    for s, k in peers:
        plane_key_copy(s, k).start()
    each_if(1, layers, sends, lambda s: column_key_copy(s, slot_of(s)).start())

    for s in near:
        plane_copy(s, first_half(s)).wait_recv()
        for t in far:
            if s == t % lows:
                relay_copy(t, 0).start()
            if s == t - t % lows:
                relay_copy(t, 1).start()

    def column_keys(key):
        key = key.T[:items]
        return key[:, 0:1], key[:, 1:2], key[:, 2:3]

    def lane_keys(blocks, i):
        return jnp.concatenate([plane_key[s, k, i:i + 1, :items] for s, k in blocks], axis=1)

    def product(rows, others):
        return lax.dot_general(
            rows, others, (((1,), (1,)), ((), ())), preferred_element_type=jnp.float32
        )

    def scaled(rows, scale):
        return (rows.astype(jnp.float32) * scale).astype(jnp.bfloat16)

    def scale_plane(s, k):
        normal[s, k] = scaled(plane[s, k], column_keys(plane_key[s, k])[2])

    def arrive(j, h):
        def wait(i):
            column_copy(1, i, h).wait_recv()
            if h == 0:
                column_key_copy(1, i).wait_recv()
        for i in range(batch):
            pl.when(filled(j * batch + i))(functools.partial(wait, j * batch + i))

    def part_product(j, h, scales):
        start, size = parts[h]
        here = slice(start, start + size)
        rows = [normal[0, 0, :, here]]
        rows += [scaled(column[j * batch + i, :, here], scales[i]) for i in range(batch)]
        return product(jnp.concatenate(rows, axis=0), normal[:, :, :, here].reshape(len(every) * items, size))

    def meet(j):
        arrive(j, 0)
        keys = [column_keys(plane_key[0, 0])] + [column_keys(column_key[j * batch + i]) for i in range(batch)]
        scales = [key[2] for key in keys[1:]]
        partial[...] = part_product(j, 0, scales)
        cluster, rank = (jnp.concatenate([key[i] for key in keys], axis=0) for i in range(2))
        plane_cluster, plane_rank = lane_keys(every, 0), lane_keys(every, 1)
        arrive(j, 1)
        scores = partial[...] + part_product(j, 1, scales)
        scores = jnp.where(cluster == plane_cluster, scores, -1.0)
        earlier = plane_rank < rank
        if batch:
            behind = jnp.where(earlier[items:], -1.0, scores[items:])
            total[0:1] = jnp.maximum(total[0:1], jnp.max(behind, axis=0, keepdims=True))
        if batches == 1:
            send_plane()
        ahead = jnp.where(earlier, scores, -1.0)
        fold = ahead[:, :LANES]
        for start in range(LANES, ahead.shape[1], LANES):
            fold = jnp.maximum(fold, ahead[:, start:start + LANES])

        def best_of(i):
            return jnp.max(fold[i * items:(i + 1) * items].T, axis=0, keepdims=True)

        for i in range(batch):
            column_res[j * batch + i, 0:1, :items] = best_of(1 + i)

            def send(slot):
                column_res_copy(slot, offset_of(slot)).start()
            pl.when(filled(j * batch + i))(functools.partial(send, j * batch + i))
        own_res[0:1, :items] = best_of(0)

    def send_plane():
        for b, (s, k) in enumerate(every):
            plane_res[s, k, 0:1, :items] = total[0:1, b * items:(b + 1) * items]
        for s, k in reversed(peers):
            plane_res_copy(s, k).start()

    pass_copy(0).wait_recv()
    for s, k in peers:
        plane_key_copy(s, k).wait_recv()
    scale_plane(0, 1)
    for s in near:
        plane_copy(s, 1 - first_half(s)).wait_recv()
        pass_copy(s).start()
        scale_plane(s, 0)
    for s in near:
        pass_copy(s).wait_recv()
        scale_plane(s, 1)
    for s in far:
        relay_copy(s, 0).wait_recv()
        relay_copy(s, 1).wait_recv()
        pass_copy(s).start()
        scale_plane(s, 0)
    for s in far:
        pass_copy(s).wait_recv()
        scale_plane(s, 1)
    if batches == 1:
        meet(0)
    else:
        each(0, batches, meet)
        send_plane()

    best = own_res[0:1, :items]
    best = jnp.maximum(best, plane_res[0, 0, 0:1, :items])
    for s, k in peers:
        plane_res_copy(s, k).wait_recv()
        best = jnp.maximum(best, plane_got[s, k, 0:1, :items])
    total[0:1, :items] = best

    def take_column(s):
        column_res_copy(0, s).wait_recv()
        total[0:1, :items] = jnp.maximum(total[0:1, :items], column_got[s, 0:1, :items])

    each_if(1, layers, sends, take_column)
    out_ref[...] = total[0:1, :items].reshape(items)

    for s in near:
        for h in range(2):
            plane_copy(s, h).wait_send()
    for s in far:
        for h in range(2):
            relay_copy(s, h).wait_send()
    for s in range(groups):
        pass_copy(s).wait_send()
    for s, k in peers:
        plane_key_copy(s, k).wait_send()
        plane_res_copy(s, k).wait_send()

    def sent_out(s):
        for h in range(2):
            column_copy(s, 0, h).wait_send()
        column_key_copy(s, 0).wait_send()

    each_if(1, layers, sends, sent_out)
    each_if(0, slots, filled, lambda j: column_res_copy(j, 1).wait_send())


def per_device(embeds, cluster, priority):
    groups, layers = lax.axis_size("grp"), lax.axis_size("dev") // 2
    slots = layers // 2
    items, width = embeds.shape
    lanes = -(-items // LANES) * LANES
    batch = batch_of(slots)
    dma = pltpu.SemaphoreType.DMA
    some = max(slots, 1)
    return pl.pallas_call(
        functools.partial(kernel, groups, layers),
        out_shape=jax.ShapeDtypeStruct((items,), jnp.float32),
        in_specs=[pl.BlockSpec(memory_space=pltpu.HBM)] * 3,
        out_specs=pl.BlockSpec(memory_space=pltpu.VMEM),
        scratch_shapes=[
            pltpu.VMEM((items, width), jnp.bfloat16),
            pltpu.VMEM((items,), jnp.int32),
            pltpu.VMEM((items,), jnp.int32),
            pltpu.VMEM((groups, 2, items, width), jnp.bfloat16),
            pltpu.VMEM((groups, 2, items, width), jnp.bfloat16),
            pltpu.VMEM((some, items, width), jnp.bfloat16),
            pltpu.VMEM((groups, 2, 8, lanes), jnp.float32),
            pltpu.VMEM((some, 8, lanes), jnp.float32),
            pltpu.VMEM((groups, 2, 8, lanes), jnp.float32),
            pltpu.VMEM((some, 8, lanes), jnp.float32),
            pltpu.VMEM((groups, 2, 8, lanes), jnp.float32),
            pltpu.VMEM((layers, 8, lanes), jnp.float32),
            pltpu.VMEM((8, groups * 2 * items), jnp.float32),
            pltpu.VMEM((8, lanes), jnp.float32),
            pltpu.VMEM(((1 + batch) * items, groups * 2 * items), jnp.float32),
            dma((3,)),
            dma((groups, 2)), dma((groups, 2)),
            dma((groups, 2)), dma((groups, 2)),
            dma((groups,)), dma((groups,)),
            dma((layers, 2)), dma((some, 2)),
            dma((groups, 2)), dma((groups, 2)),
            dma((layers,)), dma((some,)),
            dma((groups, 2)), dma((groups, 2)),
            dma((some,)), dma((layers,)),
        ],
        compiler_params=pltpu.CompilerParams(
            collective_id=0, has_side_effects=True, vmem_limit_bytes=40 * 1024 * 1024
        ),
    )(*[pltpu.with_memory_space_constraint(x, pltpu.HBM) for x in (embeds, cluster, priority)])


def solution(mesh):
    in_specs = (P(("grp", "dev"), None), P(("grp", "dev")), P(("grp", "dev")))
    out_specs = P(("grp", "dev"))
    return jax.shard_map(
        per_device, mesh=mesh, in_specs=in_specs, out_specs=out_specs, check_vma=False
    )
```

profile of v0, /device:TPU:0, one launch (start us, length us, event | category | flops | bytes accessed | tf_op | source)
XLA Modules:
  0.0 22.2 jit_solution(8996534647077806909)
XLA Ops:
  0.0 21.7 %shard_map.37 = f32[96]{0:T(128)S(1)} custom-call(bf16[96,1024]{1,0:T(8,128)(2,1)} %embeds_hbm.1, s32[96]{0:T(128)} %cluster_hbm.1, s32[96]{0:T(128)} %priority_hbm.1), custom_call_target="tpu_custom_call" | custom-call | tf_op jit(solution)/shard_map/pallas_call | solution.py:322
  21.7 0.5 %copy.5 = f32[96]{0:T(128)} copy(f32[96]{0:T(128)S(1)} %shard_map.37) | data formatting | bytes 768
where the time goes:
time: 22.3 us; the launch traced here: 22.2 us
  Pallas kernels  21.7 us (97%)
  local copies, waits for them, and re-layouts  0.51 us (2%)
    pallas_call x1, Pallas kernels, per_device(): pl.pallas_call(functools.partial(kernel, groups, layers), out_shape=jax.S...  21.7 us
    unnamed x1, local copies, waits for them, and re-layouts  0.51 us

commit v1 on v0

--- a/solution.py
+++ b/solution.py
@@ -18,7 +18,7 @@
 def kernel(
     groups, layers, embeds_hbm, cluster_hbm, priority_hbm, out_ref,
     embeds_ref, cluster_ref, priority_ref,
-    plane, normal, column, plane_key, column_key, plane_res, column_res, plane_got, column_got, total,
+    plane, column, plane_key, column_key, plane_res, column_res, plane_got, column_got, total,
     own_res, partial, load_sem, plane_send, plane_recv, relay_send, relay_recv, pass_send, pass_recv,
     column_send, column_recv, plane_key_send, plane_key_recv, column_key_send, column_key_recv,
     plane_res_send, plane_res_recv, column_res_send, column_res_recv,
@@ -94,7 +94,7 @@
         return pl.ds(h * half, half)
 
     def plane_copy(s, h):
-        return remote(embeds_hbm.at[rows_of(h)], plane.at[s, 0, rows_of(h)],
+        return remote(plane.at[0, 0, rows_of(h)], plane.at[s, 0, rows_of(h)],
                       plane_send.at[s, h], plane_recv.at[s, h], at(group_up(s), z, c))
 
     def relay_copy(s, h):
@@ -104,12 +104,12 @@
                       relay_send.at[s, h], relay_recv.at[s, h], at(group_up(way), z, c))
 
     def pass_copy(s):
-        return remote(plane.at[s, 0] if s else embeds_hbm, plane.at[s, 1],
+        return remote(plane.at[s, 0], plane.at[s, 1],
                       pass_send.at[s], pass_recv.at[s], at(g, z, core(1)))
 
     def column_copy(s, j, h):
         columns = pl.ds(*parts[h])
-        return remote(embeds_hbm.at[:, columns], column.at[j, :, columns],
+        return remote(plane.at[0, 0, :, columns], column.at[j, :, columns],
                       column_send.at[s, h], column_recv.at[j, h], at(g, layer_up(s), c))
 
     def plane_key_copy(s, k):
@@ -147,27 +147,27 @@
     for s, k in peers:
         greet(at(group_up(s), z, core(k)))
 
-    pl.semaphore_wait(barrier, len(peers) + layers - 1)
-
-    def first_half(s):
-        return 0 if s < lows else 1
-
-    for i in range(2):
-        each_if(1, layers, sends, lambda s: column_copy(s, slot_of(s), i).start())
-        for s in near:
-            plane_copy(s, first_half(s) if i == 0 else 1 - first_half(s)).start()
-    pass_copy(0).start()
-
     total[...] = jnp.full(total.shape, -1.0, jnp.float32)
     plane_key[0, 0] = jnp.full((8, lanes), -1.0, jnp.float32)
     for load in loads:
         load.wait()
     values = embeds_ref[...].astype(jnp.float32)
     scale = lax.rsqrt(jnp.sum(values * values, axis=1, keepdims=True) + 1e-06)
-    normal[0, 0] = (values * scale).astype(jnp.bfloat16)
+    plane[0, 0] = (values * scale).astype(jnp.bfloat16)
     plane_key[0, 0, 0:1, :items] = cluster_ref[...].reshape(1, items).astype(jnp.float32)
     plane_key[0, 0, 1:2, :items] = priority_ref[...].reshape(1, items).astype(jnp.float32)
-    plane_key[0, 0, 2:3, :items] = jnp.broadcast_to(scale, (items, LANES)).T[0:1]
+
+    pl.semaphore_wait(barrier, len(peers) + layers - 1)
+
+    def first_half(s):
+        return 0 if s < lows else 1
+
+    for i in range(2):
+        each_if(1, layers, sends, lambda s: column_copy(s, slot_of(s), i).start())
+        for s in near:
+            plane_copy(s, first_half(s) if i == 0 else 1 - first_half(s)).start()
+    pass_copy(0).start()
+
     for s, k in peers:
         plane_key_copy(s, k).start()
     each_if(1, layers, sends, lambda s: column_key_copy(s, slot_of(s)).start())
@@ -182,7 +182,7 @@
 
     def column_keys(key):
         key = key.T[:items]
-        return key[:, 0:1], key[:, 1:2], key[:, 2:3]
+        return key[:, 0:1], key[:, 1:2]
 
     def lane_keys(blocks, i):
         return jnp.concatenate([plane_key[s, k, i:i + 1, :items] for s, k in blocks], axis=1)
@@ -191,12 +191,6 @@
         return lax.dot_general(
             rows, others, (((1,), (1,)), ((), ())), preferred_element_type=jnp.float32
         )
-
-    def scaled(rows, scale):
-        return (rows.astype(jnp.float32) * scale).astype(jnp.bfloat16)
-
-    def scale_plane(s, k):
-        normal[s, k] = scaled(plane[s, k], column_keys(plane_key[s, k])[2])
 
     def arrive(j, h):
         def wait(i):
@@ -206,22 +200,20 @@
         for i in range(batch):
             pl.when(filled(j * batch + i))(functools.partial(wait, j * batch + i))
 
-    def part_product(j, h, scales):
+    def part_product(j, h):
         start, size = parts[h]
         here = slice(start, start + size)
-        rows = [normal[0, 0, :, here]]
-        rows += [scaled(column[j * batch + i, :, here], scales[i]) for i in range(batch)]
-        return product(jnp.concatenate(rows, axis=0), normal[:, :, :, here].reshape(len(every) * items, size))
+        rows = [plane[0, 0, :, here]] + [column[j * batch + i, :, here] for i in range(batch)]
+        return product(jnp.concatenate(rows, axis=0), plane[:, :, :, here].reshape(len(every) * items, size))
 
     def meet(j):
         arrive(j, 0)
         keys = [column_keys(plane_key[0, 0])] + [column_keys(column_key[j * batch + i]) for i in range(batch)]
-        scales = [key[2] for key in keys[1:]]
-        partial[...] = part_product(j, 0, scales)
+        partial[...] = part_product(j, 0)
         cluster, rank = (jnp.concatenate([key[i] for key in keys], axis=0) for i in range(2))
         plane_cluster, plane_rank = lane_keys(every, 0), lane_keys(every, 1)
         arrive(j, 1)
-        scores = partial[...] + part_product(j, 1, scales)
+        scores = partial[...] + part_product(j, 1)
         scores = jnp.where(cluster == plane_cluster, scores, -1.0)
         earlier = plane_rank < rank
         if batch:
@@ -254,22 +246,17 @@
     pass_copy(0).wait_recv()
     for s, k in peers:
         plane_key_copy(s, k).wait_recv()
-    scale_plane(0, 1)
     for s in near:
         plane_copy(s, 1 - first_half(s)).wait_recv()
         pass_copy(s).start()
-        scale_plane(s, 0)
     for s in near:
         pass_copy(s).wait_recv()
-        scale_plane(s, 1)
     for s in far:
         relay_copy(s, 0).wait_recv()
         relay_copy(s, 1).wait_recv()
         pass_copy(s).start()
-        scale_plane(s, 0)
     for s in far:
         pass_copy(s).wait_recv()
-        scale_plane(s, 1)
     if batches == 1:
         meet(0)
     else:
@@ -328,7 +315,6 @@
             pltpu.VMEM((items, width), jnp.bfloat16),
             pltpu.VMEM((items,), jnp.int32),
             pltpu.VMEM((items,), jnp.int32),
-            pltpu.VMEM((groups, 2, items, width), jnp.bfloat16),
             pltpu.VMEM((groups, 2, items, width), jnp.bfloat16),
             pltpu.VMEM((some, items, width), jnp.bfloat16),
             pltpu.VMEM((groups, 2, 8, lanes), jnp.float32),

time: 22.3 us -> 22 us (0.987)
  Pallas kernels: 21.7 us -> 21.4 us
    pallas_call x1, Pallas kernels: 21.7 us -> 21.4 us  [per_device(): pl.pallas_call(functools.partial(kernel, groups, layers), out_shape=jax.S...]
where the time goes in v1:
time: 22 us; the launch traced here: 21.9 us
  Pallas kernels  21.4 us (97%)
  local copies, waits for them, and re-layouts  0.51 us (2%)
    pallas_call x1, Pallas kernels, per_device(): pl.pallas_call(functools.partial(kernel, groups, layers), out_shape=jax.S...  21.4 us
    unnamed x1, local copies, waits for them, and re-layouts  0.51 us

profile of v1, /device:TPU:0, one launch (start us, length us, event | category | flops | bytes accessed | tf_op | source)
XLA Modules:
  0.0 21.9 jit_solution(4475190627094512583)
XLA Ops:
  0.0 21.4 %shard_map.37 = f32[96]{0:T(128)S(1)} custom-call(bf16[96,1024]{1,0:T(8,128)(2,1)} %embeds_hbm.1, s32[96]{0:T(128)} %cluster_hbm.1, s32[96]{0:T(128)} %priority_hbm.1), custom_call_target="tpu_custom_call" | custom-call | tf_op jit(solution)/shard_map/pallas_call | solution.py:309
  21.4 0.5 %copy.5 = f32[96]{0:T(128)} copy(f32[96]{0:T(128)S(1)} %shard_map.37) | data formatting | bytes 768
